TPU v7x, 512 devices: a whole 4x8x8 slice. The times are simulated.
512 devices in a mesh: section: 4 (over x), seq: 128 (over z, y, core).
Axes of the slice: x: 4, y: 8, z: 8, core: 2. Of those that a mesh axis runs over, the one named last changes fastest.
Arguments:
- hidden: bfloat16 [65536, 4096], P('seq', 'section'), may hold values from -6 to 6
- norm_gain: bfloat16 [4096], P('section'), may hold values from 0.25 to 1.75
- query_weight: bfloat16 [4096, 512], P(None, 'section')
- key_weight: bfloat16 [4096, 128], P('section')
- value_weight: bfloat16 [4096, 128], P('section'), may hold values from -0.5 to 0.5
- output_weight: bfloat16 [512, 4096], P(None, 'section'), may hold values from -0.25 to 0.25
- block_reach: int32 [512], P('seq'), may hold values from 0 to 2
- header_ids: int32 [2], replicated, may hold values from 0 to 511, as said below
Outputs:
- attention_out: bfloat16 [65536, 4096], P('seq', 'section')
Inputs may be any that keep to these rules, and one draw needn't show every extreme that they name: `header_ids`: the 2 indices are distinct block indices, and the last block, 511, is always one of them, at any position.
All inputs are finite; a program needn't handle non-finite values.
Results may differ from a plain program's by a relative error of at most 0.014.
Values may be sent and summed in bfloat16 or wider, within the bound.
No kernel may reach another device: no remote copies, remote signals or barrier semaphores. Data moves between devices by JAX's collectives and lax.ppermute only.
A program may use at most 64 MiB of HBM per device.

v0:
```python
import math
import jax
import jax.numpy as jnp
from jax import lax
from jax.sharding import PartitionSpec as P

BLOCK = 128
REACH = 2
EPSILON = 1e-05
THETA = 500000.0


def shift(value, axis, by):
    count = lax.axis_size(axis)
    return lax.ppermute(value, axis, [(i, (i + by) % count) for i in range(count)])


def tables(positions, head_width):
    middle = head_width // 2
    frequency = jnp.exp(
        -(2.0 / head_width) * math.log(THETA) * jnp.arange(middle, dtype=jnp.float32)
    )
    angles = positions.astype(jnp.float32)[:, None] * frequency[None, :]
    cosine, sine = (jnp.cos(angles), jnp.sin(angles))
    return (jnp.concatenate([cosine, cosine], axis=1), jnp.concatenate([-sine, sine], axis=1))


def rotate(values, cosine, signed_sine):
    middle = values.shape[-1] // 2
    turned = jnp.concatenate([values[..., middle:], values[..., :middle]], axis=-1)
    return values * cosine + turned * signed_sine


def project(total, cosine, sine, head_width):
    bf16 = jnp.bfloat16
    queries = rotate(total[:, :head_width], cosine, sine).astype(bf16)
    keys = rotate(total[:, head_width : 2 * head_width], cosine, sine).astype(bf16)
    return (queries, keys, total[:, 2 * head_width :].astype(bf16))


def on_device(
    hidden,
    norm_gain,
    query_weight,
    key_weight,
    value_weight,
    output_weight,
    block_reach,
    header_ids,
):
    bf16, f32 = (jnp.bfloat16, jnp.float32)
    rows, part = hidden.shape
    head_width = key_weight.shape[1]
    sections = lax.axis_size("section")
    shards = lax.axis_size("seq")
    local_blocks = rows // BLOCK
    total_blocks = local_blocks * shards
    section_place = lax.axis_index("section")
    seq_place = lax.axis_index("seq")
    headers = header_ids.shape[0]
    lines = BLOCK // shards
    mine = headers * lines
    owners = header_ids // local_blocks
    slots = header_ids % local_blocks
    width = part * sections
    gain = norm_gain.astype(f32)[None, :]
    candidates = jnp.concatenate(
        [
            lax.dynamic_slice_in_dim(hidden, slots[h] * BLOCK, BLOCK, axis=0).reshape(
                shards, lines, part
            )
            for h in range(headers)
        ],
        axis=1,
    )
    spread = lax.all_to_all(candidates, "seq", 0, 0)
    floats = hidden.astype(f32)
    squares = jnp.sum(floats * floats, axis=1).reshape(-1, head_width)
    squares_high = squares.astype(bf16)
    squares_low = (squares - squares_high.astype(f32)).astype(bf16)
    square_rows = squares.shape[0]
    head_weights = []
    for k in range(sections):
        target = (section_place + k) % sections
        piece = lax.dynamic_slice_in_dim(query_weight, target * part, part, axis=0)
        if k:
            piece = jnp.concatenate([piece, squares_high, squares_low])
            piece = shift(piece, "section", k)
            tail = piece[part:].astype(f32)
            squares = squares + tail[:square_rows] + tail[square_rows:]
            piece = piece[:part]
        head_weights.append(piece)
    scaling = lax.rsqrt(squares.reshape(-1) / width + EPSILON)
    normed = (floats * scaling[:, None] * gain).astype(bf16)
    header_rows = jnp.concatenate(
        [
            lax.dynamic_slice_in_dim(spread, owners[h], 1, axis=0)[0, h * lines : (h + 1) * lines]
            for h in range(headers)
        ]
    ).astype(f32)
    gained = header_rows * gain
    gained_high = gained.astype(bf16)
    gained_low = (gained - gained_high.astype(f32)).astype(bf16)
    left = jnp.concatenate([normed, gained_high, gained_low])
    header_squares = jnp.broadcast_to(
        jnp.sum(header_rows * header_rows, axis=1, keepdims=True), (mine, head_width)
    )
    products = [
        jnp.dot(left, weight, preferred_element_type=f32)
        for weight in head_weights + [key_weight, value_weight]
    ]
    mains = [value[:rows].astype(bf16) for value in products]
    smalls = [value[rows : rows + mine] + value[rows + mine :] for value in products]
    highs = [value.astype(bf16) for value in smalls + [header_squares]]
    lows = [
        (value - high.astype(f32)).astype(bf16)
        for value, high in zip(smalls + [header_squares], highs)
    ]
    used = 3 * rows + 8 * mine
    filler = jnp.zeros((-used % BLOCK, head_width), bf16)
    chunks = []
    for target in range(sections):
        which = (section_place - target) % sections

        def chosen(options):
            value = options[0]
            for k in range(1, sections):
                value = jnp.where(which == k, options[k], value)
            return value

        chunks.append(
            jnp.concatenate(
                [chosen(mains), mains[sections], mains[sections + 1]]
                + [chosen(highs)]
                + highs[sections:]
                + [chosen(lows)]
                + lows[sections:]
                + [filler]
            )
        )
    arrived = lax.all_to_all(jnp.stack(chunks), "section", 0, 0)
    total = jnp.sum(arrived[:, :used].astype(f32), axis=0)
    small = total[3 * rows :]
    small = (small[: 4 * mine] + small[4 * mine :]).reshape(4, mine, head_width)
    small = small[:3] * lax.rsqrt(small[3] / width + EPSILON)
    total = jnp.concatenate([total[k * rows : (k + 1) * rows] for k in range(3)], axis=1)
    header_total = jnp.concatenate([small[0], small[1], small[2]], axis=1)
    header_positions = (
        header_ids[:, None] * BLOCK + seq_place * lines + jnp.arange(lines, dtype=jnp.int32)[None]
    ).reshape(-1)
    header_chunk = jnp.concatenate(
        project(header_total, *tables(header_positions, head_width), head_width), axis=1
    )
    header_pack = lax.all_to_all(
        jnp.broadcast_to(header_chunk[None], (shards,) + header_chunk.shape), "seq", 0, 0
    ).reshape(-1, 3 * head_width)
    own_positions = seq_place * rows + jnp.arange(rows, dtype=jnp.int32)
    queries, keys, values = project(total, *tables(own_positions, head_width), head_width)
    stacked = jnp.concatenate([keys, values], axis=1)
    head_queries = header_pack[:, :head_width]
    head_keys = header_pack[:, head_width : 2 * head_width]
    head_values = header_pack[:, 2 * head_width :]
    inverse_root = 1.0 / math.sqrt(head_width)
    far_scores = (
        jnp.einsum("qd,kd->qk", head_queries, keys, preferred_element_type=f32) * inverse_root
    )
    far_max = jnp.max(far_scores, axis=1, keepdims=True)
    far_weights = jnp.exp(far_scores - far_max)
    far_total = jnp.sum(far_weights, axis=1, keepdims=True)
    far_out = jnp.dot(far_weights.astype(bf16), values, preferred_element_type=f32) / far_total
    far_level = far_max + jnp.log(far_total)
    first = far_level.astype(bf16).astype(f32)
    second = (far_level - first).astype(bf16).astype(f32)
    third = far_level - first - second
    lane = lax.broadcasted_iota(jnp.int32, far_out.shape, 1)
    level = jnp.where(lane < 32, first, jnp.where(lane < 64, second, third))
    partial = jnp.concatenate([far_out, level], axis=1).astype(bf16)
    partial, queries = lax.optimization_barrier((partial, queries))
    parts = lax.all_to_all(partial.reshape(shards, mine, 2 * head_width), "seq", 0, 0)
    parts = parts.astype(f32)
    levels = sum((parts[..., head_width + lane : head_width + lane + 1] for lane in (0, 32, 64)))
    factor = jnp.exp(levels - jnp.max(levels, axis=0, keepdims=True))
    header_result = jnp.sum(parts[..., :head_width] * factor, axis=0) / jnp.sum(factor, axis=0)
    header_all = lax.all_to_all(
        jnp.broadcast_to(header_result.astype(bf16)[None], (shards, mine, head_width)), "seq", 0, 0
    ).reshape(shards, headers, lines, head_width)
    margin_rows = REACH * BLOCK
    extended = jnp.concatenate(
        [
            shift(stacked[rows - margin_rows :], "seq", 1),
            stacked,
            shift(stacked[:margin_rows], "seq", -1),
        ]
    )
    near_keys = extended[:, :head_width]
    near_values = extended[:, head_width:]
    extent = rows + 2 * margin_rows
    key_blocks = seq_place * local_blocks - REACH + jnp.arange(extent, dtype=jnp.int32) // BLOCK
    query_blocks = seq_place * local_blocks + jnp.arange(rows, dtype=jnp.int32) // BLOCK
    limits = jnp.repeat(block_reach, BLOCK)
    key_header = jnp.any(header_ids[:, None] == key_blocks[None, :], axis=0)
    allowed = (key_blocks >= 0)[None, :] & (key_blocks < total_blocks)[None, :]
    allowed = allowed & (jnp.abs(key_blocks[None, :] - query_blocks[:, None]) <= limits[:, None])
    allowed = allowed & jnp.logical_not(key_header)[None, :]
    near_scores = (
        jnp.einsum("qd,kd->qk", queries, near_keys, preferred_element_type=f32) * inverse_root
    )
    near_scores = jnp.where(allowed, near_scores, -jnp.inf)
    head_scores = (
        jnp.einsum("qd,kd->qk", queries, head_keys, preferred_element_type=f32) * inverse_root
    )
    scores = jnp.concatenate([near_scores, head_scores], axis=1)
    row_top = jnp.max(scores, axis=1)
    weights = jnp.exp(scores - row_top[:, None])
    row_sums = jnp.sum(weights, axis=1)
    joined = jnp.concatenate([near_values, head_values], axis=0)
    mixed = (
        jnp.dot(weights.astype(bf16), joined, preferred_element_type=f32) / row_sums[:, None]
    ).astype(bf16)
    blocks = []
    for b in range(local_blocks):
        block = mixed[b * BLOCK : (b + 1) * BLOCK]
        for h in range(headers):
            here = header_ids[h] == seq_place * local_blocks + b
            block = jnp.where(here, header_all[:, h].reshape(BLOCK, head_width), block)
        blocks.append(block)
    attended = jnp.concatenate(blocks, axis=0)
    gathered = lax.all_gather(attended, "section", axis=1, tiled=True)
    return jnp.dot(gathered, output_weight, preferred_element_type=f32).astype(bf16)


def solution(mesh):
    return jax.shard_map(
        on_device,
        mesh=mesh,
        in_specs=(
            P("seq", "section"),
            P("section"),
            P(None, "section"),
            P("section", None),
            P("section", None),
            P(None, "section"),
            P("seq"),
            P(),
        ),
        out_specs=P("seq", "section"),
        check_vma=False,
    )
```

profile of v0, /device:TPU:2, one launch (start us, length us, event | category | flops | bytes accessed | tf_op | source)
XLA Modules:
  0.0 179.3 jit_solution(14884136693440306708)
XLA Ops:
  0.1 1.6 fusion.1
  1.7 1.2 constant_dynamic-slice_fusion.2
  3.0 7.8 %collective-permute-start.2 = (bf16[1032,128]{1,0:T(8,128)(2,1)S(1)}, bf16[1032,128]{1,0:T(8,128)(2,1)}, u32[]{:S(2)}, u32[]{:S(2)}) collective-permute-start(bf16[1032,128]{1,0:T(8,128)(2,1)S(1)} %concatenate.78), channel_id=1, source_target_pairs={{0,384},{128,0},{256,128},{384,256},{1,385},{129,1},{257,129},{385... | collective-permute-start | bytes 792584 | tf_op jit(solution)/shard_map/ppermute | solution.py:15
  11.0 1.9 %collective-permute-start.1 = (bf16[1032,128]{1,0:T(8,128)(2,1)S(1)}, bf16[1032,128]{1,0:T(8,128)(2,1)}, u32[]{:S(2)}, u32[]{:S(2)}) collective-permute-start(bf16[1032,128]{1,0:T(8,128)(2,1)S(1)} %concatenate.77), channel_id=1, source_target_pairs={{0,256},{128,384},{256,0},{384,128},{1,257},{129,385},{257,1},{385... | collective-permute-start | bytes 792584 | tf_op jit(solution)/shard_map/ppermute | solution.py:15
  15.3 1.3 copy.27
  16.7 15.4 %all-to-all-start = ((bf16[128,2,1024]{2,1,0:T(2,128)(2,1)}), bf16[128,2,1024]{2,1,0:T(2,128)(2,1)}, u32[]{:S(2)}, u32[]{:S(2)}) async-start(bf16[128,2,1024]{2,1,0:T(2,128)(2,1)} %copy.27), calls=%async_computation | async-start | bytes 1048576 | tf_op jit(solution)/shard_map/all_to_all | solution.py:76
  32.2 3.7 %collective-permute-start = (bf16[1032,128]{1,0:T(8,128)(2,1)S(1)}, bf16[1032,128]{1,0:T(8,128)(2,1)}, u32[]{:S(2)}, u32[]{:S(2)}) collective-permute-start(bf16[1032,128]{1,0:T(8,128)(2,1)S(1)} %concatenate.76), channel_id=1, source_target_pairs={{0,128},{128,256},{256,384},{384,0},{1,129},{129,257},{257,385},{3... | collective-permute-start | bytes 792584 | tf_op jit(solution)/shard_map/ppermute | solution.py:15
  40.9 1.1 collective-permute-done
  43.0 7.9 %all-to-all-done = bf16[128,2,1024]{2,1,0:T(2,128)(2,1)} async-done(((bf16[128,2,1024]{2,1,0:T(2,128)(2,1)}), bf16[128,2,1024]{2,1,0:T(2,128)(2,1)}, u32[]{:S(2)}, u32[]{:S(2)}) %all-to-all-start) | async-done | bytes 524320 | tf_op jit(solution)/shard_map/all_to_all | solution.py:76
  51.8 1.4 fusion.35
  53.2 1.4 fusion.28
  54.6 1.4 fusion.30
  56.0 1.4 fusion.32
  59.9 1.4 pad_maximum_fusion
  61.4 5.3 %all-to-all-start.1 = ((bf16[4,1664,128]{2,1,0:T(8,128)(2,1)}), bf16[4,1664,128]{2,1,0:T(8,128)(2,1)S(1)}, u32[]{:S(2)}, u32[]{:S(2)}) async-start(bf16[4,1664,128]{2,1,0:T(8,128)(2,1)} %pad_maximum_fusion), calls=%async_computation.1 | async-start | bytes 3407872 | tf_op jit(solution)/shard_map/all_to_all | solution.py:141
  69.8 1.9 %fusion.39 = (f32[512,64]{1,0:T(8,128)}, f32[512,64]{1,0:T(8,128)}, f32[512,64]{1,0:T(8,128)}) fusion(f32[64]{0:T(128)S(1)} %multiply_exponential_fusion, f32[512]{0:T(512)S(1)} %add_convert_fusion), kind=kLoop, calls=%fused_computation.79 | loop fusion | flops 65536 | bytes 395520 | tf_op jit(solution)/shard_map/neg | solution.py:25
  71.7 16.7 %all-to-all-done.1 = bf16[4,1664,128]{2,1,0:T(8,128)(2,1)S(1)} async-done(((bf16[4,1664,128]{2,1,0:T(8,128)(2,1)}), bf16[4,1664,128]{2,1,0:T(8,128)(2,1)S(1)}, u32[]{:S(2)}, u32[]{:S(2)}) %all-to-all-start.1) | async-done | bytes 1703968 | tf_op jit(solution)/shard_map/all_to_all | solution.py:141
  91.4 7.2 %all-to-all-start.2 = ((bf16[128,2,384]{2,1,0:T(2,128)(2,1)}), bf16[128,2,384]{2,1,0:T(2,128)(2,1)}, u32[]{:S(2)}, u32[]{:S(2)}) async-start(bf16[128,2,384]{2,1,0:T(2,128)(2,1)} %broadcast_in_dim.42), calls=%async_computation.2 | async-start | bytes 393216 | tf_op jit(solution)/shard_map/all_to_all | solution.py:154
  98.7 1.4 fusion.25
  100.1 6.8 %collective-permute-start.4 = (bf16[256,256]{1,0:T(8,128)(2,1)S(1)}, bf16[256,256]{1,0:T(8,128)(2,1)S(1)}, u32[]{:S(2)}, u32[]{:S(2)}) collective-permute-start(bf16[256,256]{1,0:T(8,128)(2,1)S(1)} %get-tuple-element.52), channel_id=1, source_target_pairs={{0,127},{1,0},{2,1},{3,2},{4,3},{5,4},{6,5},{7,6},{8,7},{9,8},{10,... | collective-permute-start | bytes 393224 | tf_op jit(solution)/shard_map/ppermute | solution.py:15
  106.9 2.1 %collective-permute-start.3 = (bf16[256,256]{1,0:T(8,128)(2,1)S(1)}, bf16[256,256]{1,0:T(8,128)(2,1)S(1)}, u32[]{:S(2)}, u32[]{:S(2)}) collective-permute-start(bf16[256,256]{1,0:T(8,128)(2,1)S(1)} %get-tuple-element.51), channel_id=1, source_target_pairs={{0,1},{1,2},{2,3},{3,4},{4,5},{5,6},{6,7},{7,8},{8,9},{9,10},{10,1... | collective-permute-start | bytes 393224 | tf_op jit(solution)/shard_map/ppermute | solution.py:15
  114.4 2.1 %collective-permute-done.3 = bf16[256,256]{1,0:T(8,128)(2,1)S(1)} collective-permute-done((bf16[256,256]{1,0:T(8,128)(2,1)S(1)}, bf16[256,256]{1,0:T(8,128)(2,1)S(1)}, u32[]{:S(2)}, u32[]{:S(2)}) %collective-permute-start.3) | collective-permute-done | bytes 131104 | tf_op jit(solution)/shard_map/ppermute | solution.py:15
  118.1 1.0 reshape.162
  120.9 8.7 %all-to-all-start.3 = ((bf16[128,2,256]{2,1,0:T(2,128)(2,1)}), bf16[128,2,256]{2,1,0:T(2,128)(2,1)}, u32[]{:S(2)}, u32[]{:S(2)}) async-start(bf16[128,2,256]{2,1,0:T(2,128)(2,1)} %reshape.163), calls=%async_computation.3 | async-start | bytes 262144 | tf_op jit(solution)/shard_map/all_to_all | solution.py:179
  129.7 2.0 %fusion.102 = (f32[512]{0:T(512)S(1)}, f32[512,1024]{1,0:T(8,128)S(1)}) fusion(bf16[512,128]{1,0:T(8,128)(2,1)S(1)} %get-tuple-element.8, bf16[1024,256]{1,0:T(8,128)(2,1)} %copy-done.3, pred[1024]{0:T(1024)(128)(4,1)S(1)} %not.7, s32[512]{0:T(512)S(1)} %copy-done.11, s32[512]{0:T(512)S(1)} %fusion.54, s32[1024]{0:T(1024)S(1)} %fusion.50, ...), kind=kOutput, calls=%fused_computation.232 | convolution fusion | flops 138411520 | bytes 2502656 | tf_op jit(solution)/shard_map/qd,kd->qk/dot_general | solution.py:206
  133.3 8.1 %all-to-all-done.3 = bf16[128,2,256]{2,1,0:T(2,128)(2,1)} async-done(((bf16[128,2,256]{2,1,0:T(2,128)(2,1)}), bf16[128,2,256]{2,1,0:T(2,128)(2,1)}, u32[]{:S(2)}, u32[]{:S(2)}) %all-to-all-start.3) | async-done | bytes 131104 | tf_op jit(solution)/shard_map/all_to_all | solution.py:179
  141.4 1.0 convert_element_type.263
  145.9 6.1 %all-to-all-start.4 = ((bf16[128,2,128]{2,1,0:T(2,128)(2,1)}), bf16[128,2,128]{2,1,0:T(2,128)(2,1)S(1)}, u32[]{:S(2)}, u32[]{:S(2)}) async-start(bf16[128,2,128]{2,1,0:T(2,128)(2,1)} %broadcast_in_dim.46), calls=%async_computation.4 | async-start | bytes 131072 | tf_op jit(solution)/shard_map/all_to_all | solution.py:184
  152.0 1.7 fusion.13
  153.7 9.4 %all-to-all-done.4 = bf16[128,2,128]{2,1,0:T(2,128)(2,1)S(1)} async-done(((bf16[128,2,128]{2,1,0:T(2,128)(2,1)}), bf16[128,2,128]{2,1,0:T(2,128)(2,1)S(1)}, u32[]{:S(2)}, u32[]{:S(2)}) %all-to-all-start.4) | async-done | bytes 65568 | tf_op jit(solution)/shard_map/all_to_all | solution.py:184
  163.2 14.4 %all_gather.3 = bf16[512,512]{1,0:T(8,128)(2,1)S(1)} all-gather(bf16[512,128]{1,0:T(8,128)(2,1)S(1)} %pad_maximum_fusion.8), channel_id=1, replica_groups=mesh['section'=4,'seq'=128] {'section'}, dimensions={1}, use_global_device_ids=true | all-gather | bytes 655360 | tf_op jit(solution)/shard_map/all_gather | solution.py:228
  177.6 1.7 convolution_convert_fusion
  (129 shorter events, 22.6 us)
Async XLA Ops:
  0.0 177.6 %copy-start = (bf16[512,1024]{1,0:T(8,128)(2,1)S(1)}, bf16[512,1024]{1,0:T(8,128)(2,1)}, u32[]{:S(2)}) copy-start(bf16[512,1024]{1,0:T(8,128)(2,1)} %param.13) | copy-start | bytes 3145732
  0.0 15.2 %copy-start.1 = (bf16[512,1024]{1,0:T(8,128)(2,1)S(1)}, bf16[512,1024]{1,0:T(8,128)(2,1)}, u32[]{:S(2)}) copy-start(bf16[512,1024]{1,0:T(8,128)(2,1)} %param.8) | copy-start | bytes 3145732
  0.0 12.9 %copy-start.9 = (s32[2]{0:T(128)S(1)}, s32[2]{0:T(128)}, u32[]{:S(2)}) copy-start(s32[2]{0:T(128)} %param.15) | copy-start | bytes 28
  3.0 36.5 %collective-permute-start.2 = (bf16[1032,128]{1,0:T(8,128)(2,1)S(1)}, bf16[1032,128]{1,0:T(8,128)(2,1)}, u32[]{:S(2)}, u32[]{:S(2)}) collective-permute-start(bf16[1032,128]{1,0:T(8,128)(2,1)S(1)} %concatenate.78), channel_id=1, source_target_pairs={{0,384},{128,0},{256,128},{384,256},{1,385},{129,1},{257,129},{385... | collective-permute-start | bytes 792584 | tf_op jit(solution)/shard_map/ppermute | solution.py:15
  11.0 29.2 %collective-permute-start.1 = (bf16[1032,128]{1,0:T(8,128)(2,1)S(1)}, bf16[1032,128]{1,0:T(8,128)(2,1)}, u32[]{:S(2)}, u32[]{:S(2)}) collective-permute-start(bf16[1032,128]{1,0:T(8,128)(2,1)S(1)} %concatenate.77), channel_id=1, source_target_pairs={{0,256},{128,384},{256,0},{384,128},{1,257},{129,385},{257,1},{385... | collective-permute-start | bytes 792584 | tf_op jit(solution)/shard_map/ppermute | solution.py:15
  15.3 23.1 %copy-start.10 = (bf16[1024]{0:T(1024)(128)(2,1)S(1)}, bf16[1024]{0:T(1024)(128)(2,1)}, u32[]{:S(2)}) copy-start(bf16[1024]{0:T(1024)(128)(2,1)} %param.9) | copy-start | bytes 6148
  16.7 34.3 %all-to-all-start = ((bf16[128,2,1024]{2,1,0:T(2,128)(2,1)}), bf16[128,2,1024]{2,1,0:T(2,128)(2,1)}, u32[]{:S(2)}, u32[]{:S(2)}) async-start(bf16[128,2,1024]{2,1,0:T(2,128)(2,1)} %copy.27), calls=%async_computation | async-start | bytes 1048576 | tf_op jit(solution)/shard_map/all_to_all | solution.py:76
  32.2 9.8 %collective-permute-start = (bf16[1032,128]{1,0:T(8,128)(2,1)S(1)}, bf16[1032,128]{1,0:T(8,128)(2,1)}, u32[]{:S(2)}, u32[]{:S(2)}) collective-permute-start(bf16[1032,128]{1,0:T(8,128)(2,1)S(1)} %concatenate.76), channel_id=1, source_target_pairs={{0,128},{128,256},{256,384},{384,0},{1,129},{129,257},{257,385},{3... | collective-permute-start | bytes 792584 | tf_op jit(solution)/shard_map/ppermute | solution.py:15
  56.0 1.6 copy-start.16
  57.6 1.0 copy-start.17
  61.4 7.1 %copy-start.15 = (s32[4]{0:T(128)S(1)}, s32[4]{0:T(128)}, u32[]{:S(2)}) copy-start(s32[4]{0:T(128)} %param.14) | copy-start | bytes 52
  61.4 7.8 %copy-start.12 = (f32[2]{0:T(128)S(1)}, f32[2]{0:T(128)}, u32[]{:S(2)}) copy-start(f32[2]{0:T(128)} %get-tuple-element.83) | copy-start | bytes 28
  61.4 27.0 %all-to-all-start.1 = ((bf16[4,1664,128]{2,1,0:T(8,128)(2,1)}), bf16[4,1664,128]{2,1,0:T(8,128)(2,1)S(1)}, u32[]{:S(2)}, u32[]{:S(2)}) async-start(bf16[4,1664,128]{2,1,0:T(8,128)(2,1)} %pad_maximum_fusion), calls=%async_computation.1 | async-start | bytes 3407872 | tf_op jit(solution)/shard_map/all_to_all | solution.py:141
  88.6 10.0 %copy-start.4 = (f32[512,64]{1,0:T(8,128)S(1)}, f32[512,64]{1,0:T(8,128)}, u32[]{:S(2)}) copy-start(f32[512,64]{1,0:T(8,128)} %get-tuple-element.62) | copy-start | bytes 393220
  88.6 10.0 %copy-start.5 = (f32[512,64]{1,0:T(8,128)S(1)}, f32[512,64]{1,0:T(8,128)}, u32[]{:S(2)}) copy-start(f32[512,64]{1,0:T(8,128)} %get-tuple-element.63) | copy-start | bytes 393220
  88.6 10.0 %copy-start.6 = (f32[512,64]{1,0:T(8,128)S(1)}, f32[512,64]{1,0:T(8,128)}, u32[]{:S(2)}) copy-start(f32[512,64]{1,0:T(8,128)} %get-tuple-element.64) | copy-start | bytes 393220
  91.4 26.6 %all-to-all-start.2 = ((bf16[128,2,384]{2,1,0:T(2,128)(2,1)}), bf16[128,2,384]{2,1,0:T(2,128)(2,1)}, u32[]{:S(2)}, u32[]{:S(2)}) async-start(bf16[128,2,384]{2,1,0:T(2,128)(2,1)} %broadcast_in_dim.42), calls=%async_computation.2 | async-start | bytes 393216 | tf_op jit(solution)/shard_map/all_to_all | solution.py:154
  100.1 19.9 %copy-start.13 = (pred[128]{0:T(512)(128)(4,1)S(1)}, pred[128]{0:T(512)(128)(4,1)}, u32[]{:S(2)}) copy-start(pred[128]{0:T(512)(128)(4,1)} %get-tuple-element.100) | copy-start | bytes 388
  100.1 19.9 %copy-start.14 = (pred[128]{0:T(512)(128)(4,1)S(1)}, pred[128]{0:T(512)(128)(4,1)}, u32[]{:S(2)}) copy-start(pred[128]{0:T(512)(128)(4,1)} %get-tuple-element.101) | copy-start | bytes 388
  100.1 14.3 %collective-permute-start.4 = (bf16[256,256]{1,0:T(8,128)(2,1)S(1)}, bf16[256,256]{1,0:T(8,128)(2,1)S(1)}, u32[]{:S(2)}, u32[]{:S(2)}) collective-permute-start(bf16[256,256]{1,0:T(8,128)(2,1)S(1)} %get-tuple-element.52), channel_id=1, source_target_pairs={{0,127},{1,0},{2,1},{3,2},{4,3},{5,4},{6,5},{7,6},{8,7},{9,8},{10,... | collective-permute-start | bytes 393224 | tf_op jit(solution)/shard_map/ppermute | solution.py:15
  106.9 9.6 %collective-permute-start.3 = (bf16[256,256]{1,0:T(8,128)(2,1)S(1)}, bf16[256,256]{1,0:T(8,128)(2,1)S(1)}, u32[]{:S(2)}, u32[]{:S(2)}) collective-permute-start(bf16[256,256]{1,0:T(8,128)(2,1)S(1)} %get-tuple-element.51), channel_id=1, source_target_pairs={{0,1},{1,2},{2,3},{3,4},{4,5},{5,6},{6,7},{7,8},{8,9},{9,10},{10,1... | collective-permute-start | bytes 393224 | tf_op jit(solution)/shard_map/ppermute | solution.py:15
  116.6 0.8 copy-start.3
  117.4 12.3 %copy-start.11 = (s32[512]{0:T(512)S(1)}, s32[512]{0:T(512)}, u32[]{:S(2)}) copy-start(s32[512]{0:T(512)} %broadcast_bitcast_fusion) | copy-start | bytes 6148
  119.1 1.9 %copy-start.7 = (bf16[256,384]{1,0:T(8,128)(2,1)}, bf16[256,384]{1,0:T(8,128)(2,1)S(1)}, u32[]{:S(2)}) copy-start(bf16[256,384]{1,0:T(8,128)(2,1)S(1)} %reshape.162) | copy-start | bytes 589828
  120.9 20.5 %all-to-all-start.3 = ((bf16[128,2,256]{2,1,0:T(2,128)(2,1)}), bf16[128,2,256]{2,1,0:T(2,128)(2,1)}, u32[]{:S(2)}, u32[]{:S(2)}) async-start(bf16[128,2,256]{2,1,0:T(2,128)(2,1)} %reshape.163), calls=%async_computation.3 | async-start | bytes 262144 | tf_op jit(solution)/shard_map/all_to_all | solution.py:179
  129.6 2.0 %copy-start.8 = (bf16[256,384]{1,0:T(8,128)(2,1)S(1)}, bf16[256,384]{1,0:T(8,128)(2,1)}, u32[]{:S(2)}) copy-start(bf16[256,384]{1,0:T(8,128)(2,1)} %copy-done.7) | copy-start | bytes 589828
  132.0 0.8 copy-start.2
  132.8 19.2 %slice-start = ((bf16[256,384]{1,0:T(8,128)(2,1)}), bf16[256,128]{1,0:T(8,128)(2,1)S(1)}, s32[]{:S(2)}) async-start(bf16[256,384]{1,0:T(8,128)(2,1)} %copy-done.7), calls=%async_computation.5 | async-start | bytes 131072 | tf_op jit(solution)/shard_map/slice | solution.py:162
  145.9 17.2 %all-to-all-start.4 = ((bf16[128,2,128]{2,1,0:T(2,128)(2,1)}), bf16[128,2,128]{2,1,0:T(2,128)(2,1)S(1)}, u32[]{:S(2)}, u32[]{:S(2)}) async-start(bf16[128,2,128]{2,1,0:T(2,128)(2,1)} %broadcast_in_dim.46), calls=%async_computation.4 | async-start | bytes 131072 | tf_op jit(solution)/shard_map/all_to_all | solution.py:184
where the time goes:
time: 180 us; the launch traced here: 179 us
  starting transfers between devices  64.9 us (36%)
  waiting for transfers between devices  45.4 us (25%)
  other arithmetic  17.1 us (10%)
  local copies, waits for them, and re-layouts  14.5 us (8%)
  blocking collectives  14.4 us (8%)
  matrix products  12.9 us (7%)
  between operations  10.1 us (6%)
    ppermute x5, starting transfers between devices, shift(): lax.ppermute(value, axis, [(i, (i + by) % count) for i in range(count)])  22.3 us
    all_to_all x1, waiting for transfers between devices, on_device(): arrived = lax.all_to_all(jnp.stack(chunks), 'section', 0, 0)  16.7 us
    all_to_all x1, starting transfers between devices, on_device(): spread = lax.all_to_all(candidates, 'seq', 0, 0)  15.4 us
    all_gather x1, blocking collectives, on_device(): gathered = lax.all_gather(attended, 'section', axis=1, tiled=True)  14.4 us
    all_to_all x1, waiting for transfers between devices, on_device(): lax.all_to_all(jnp.broadcast_to(header_result.astype(bf16)[None], (shards...  9.42 us
    all_to_all x1, starting transfers between devices, on_device(): lax.all_to_all(partial.reshape(shards, mine, 2 * head_width), 'seq', 0, 0)  8.69 us
    all_to_all x1, waiting for transfers between devices, on_device(): lax.all_to_all(partial.reshape(shards, mine, 2 * head_width), 'seq', 0, 0)  8.1 us
    all_to_all x1, waiting for transfers between devices, on_device(): spread = lax.all_to_all(candidates, 'seq', 0, 0)  7.9 us
  transfers between devices with their start and end apart: 10, of which 6 were waited for; matrix products, arithmetic and copies ran while one was open for 10% of the time, Pallas kernels for 0%

commit v1 on v0

--- a/solution.py
+++ b/solution.py
@@ -225,7 +225,9 @@
             block = jnp.where(here, header_all[:, h].reshape(BLOCK, head_width), block)
         blocks.append(block)
     attended = jnp.concatenate(blocks, axis=0)
-    gathered = lax.all_gather(attended, "section", axis=1, tiled=True)
+    gathered = jnp.concatenate(
+        lax.all_to_all(jnp.stack([attended] * lax.axis_size("section")), "section", 0, 0), axis=1
+    )
     return jnp.dot(gathered, output_weight, preferred_element_type=f32).astype(bf16)
 
 

time: 180 us -> 179 us (level)
  the two profiles are of different devices: /device:TPU:2 before, /device:TPU:1 now
where the time goes in v1:
time: 179 us; the launch traced here: 178 us
  starting transfers between devices  64.7 us (36%)
  waiting for transfers between devices  47.5 us (27%)
  other arithmetic  17.1 us (10%)
  local copies, waits for them, and re-layouts  14.6 us (8%)
  matrix products  12.9 us (7%)
  blocking collectives  11.4 us (6%)
  between operations  10.1 us (6%)
    all_to_all x1, starting transfers between devices, on_device(): spread = lax.all_to_all(candidates, 'seq', 0, 0)  18.6 us
    all_to_all x1, waiting for transfers between devices, on_device(): arrived = lax.all_to_all(jnp.stack(chunks), 'section', 0, 0)  17.3 us
    ppermute x5, starting transfers between devices, shift(): lax.ppermute(value, axis, [(i, (i + by) % count) for i in range(count)])  15.9 us
    all_to_all x1, starting transfers between devices, on_device(): lax.all_to_all(partial.reshape(shards, mine, 2 * head_width), 'seq', 0, 0)  14.1 us
    all_to_all x1, blocking collectives, on_device(): lax.all_to_all(jnp.stack([attended] * lax.axis_size('section')), 'section...  11.4 us
    all_to_all x1, waiting for transfers between devices, on_device(): lax.all_to_all(jnp.broadcast_to(header_result.astype(bf16)[None], (shards...  9.86 us
    all_to_all x1, waiting for transfers between devices, on_device(): spread = lax.all_to_all(candidates, 'seq', 0, 0)  8.98 us
    all_to_all x1, waiting for transfers between devices, on_device(): lax.all_to_all(partial.reshape(shards, mine, 2 * head_width), 'seq', 0, 0)  8.68 us
  transfers between devices with their start and end apart: 10, of which 5 were waited for; matrix products, arithmetic and copies ran while one was open for 10% of the time, Pallas kernels for 0%

profile of v1, /device:TPU:1, one launch (start us, length us, event | category | flops | bytes accessed | tf_op | source)
XLA Modules:
  0.0 178.3 jit_solution(3130387748480801755)
XLA Ops:
  0.1 1.6 fusion.1
  1.7 1.2 constant_dynamic-slice_fusion.2
  3.0 5.2 %collective-permute-start.2 = (bf16[1032,128]{1,0:T(8,128)(2,1)S(1)}, bf16[1032,128]{1,0:T(8,128)(2,1)}, u32[]{:S(2)}, u32[]{:S(2)}) collective-permute-start(bf16[1032,128]{1,0:T(8,128)(2,1)S(1)} %concatenate.78), channel_id=1, source_target_pairs={{0,384},{128,0},{256,128},{384,256},{1,385},{129,1},{257,129},{385... | collective-permute-start | bytes 792584 | tf_op jit(solution)/shard_map/ppermute | solution.py:15
  8.4 2.4 %collective-permute-start.1 = (bf16[1032,128]{1,0:T(8,128)(2,1)S(1)}, bf16[1032,128]{1,0:T(8,128)(2,1)}, u32[]{:S(2)}, u32[]{:S(2)}) collective-permute-start(bf16[1032,128]{1,0:T(8,128)(2,1)S(1)} %concatenate.77), channel_id=1, source_target_pairs={{0,256},{128,384},{256,0},{384,128},{1,257},{129,385},{257,1},{385... | collective-permute-start | bytes 792584 | tf_op jit(solution)/shard_map/ppermute | solution.py:15
  13.3 1.3 copy.31
  14.6 18.6 %all-to-all-start = ((bf16[128,2,1024]{2,1,0:T(2,128)(2,1)}), bf16[128,2,1024]{2,1,0:T(2,128)(2,1)}, u32[]{:S(2)}, u32[]{:S(2)}) async-start(bf16[128,2,1024]{2,1,0:T(2,128)(2,1)} %copy.31), calls=%async_computation | async-start | bytes 1048576 | tf_op jit(solution)/shard_map/all_to_all | solution.py:76
  33.4 2.5 %collective-permute-start = (bf16[1032,128]{1,0:T(8,128)(2,1)S(1)}, bf16[1032,128]{1,0:T(8,128)(2,1)}, u32[]{:S(2)}, u32[]{:S(2)}) collective-permute-start(bf16[1032,128]{1,0:T(8,128)(2,1)S(1)} %concatenate.76), channel_id=1, source_target_pairs={{0,128},{128,256},{256,384},{384,0},{1,129},{129,257},{257,385},{3... | collective-permute-start | bytes 792584 | tf_op jit(solution)/shard_map/ppermute | solution.py:15
  40.8 2.6 %collective-permute-done = bf16[1032,128]{1,0:T(8,128)(2,1)} collective-permute-done((bf16[1032,128]{1,0:T(8,128)(2,1)S(1)}, bf16[1032,128]{1,0:T(8,128)(2,1)}, u32[]{:S(2)}, u32[]{:S(2)}) %collective-permute-start) | collective-permute-done | bytes 264224 | tf_op jit(solution)/shard_map/ppermute | solution.py:15
  44.5 9.0 %all-to-all-done = bf16[128,2,1024]{2,1,0:T(2,128)(2,1)} async-done(((bf16[128,2,1024]{2,1,0:T(2,128)(2,1)}), bf16[128,2,1024]{2,1,0:T(2,128)(2,1)}, u32[]{:S(2)}, u32[]{:S(2)}) %all-to-all-start) | async-done | bytes 524320 | tf_op jit(solution)/shard_map/all_to_all | solution.py:76
  54.3 1.4 fusion.35
  55.7 1.4 fusion.28
  57.1 1.4 fusion.30
  58.5 1.4 fusion.32
  62.4 1.4 pad_maximum_fusion
  63.9 3.8 %all-to-all-start.1 = ((bf16[4,1664,128]{2,1,0:T(8,128)(2,1)}), bf16[4,1664,128]{2,1,0:T(8,128)(2,1)S(1)}, u32[]{:S(2)}, u32[]{:S(2)}) async-start(bf16[4,1664,128]{2,1,0:T(8,128)(2,1)} %pad_maximum_fusion), calls=%async_computation.1 | async-start | bytes 3407872 | tf_op jit(solution)/shard_map/all_to_all | solution.py:141
  70.9 1.9 %fusion.39 = (f32[512,64]{1,0:T(8,128)}, f32[512,64]{1,0:T(8,128)}, f32[512,64]{1,0:T(8,128)}) fusion(f32[64]{0:T(128)S(1)} %multiply_exponential_fusion, f32[512]{0:T(512)S(1)} %add_convert_fusion), kind=kLoop, calls=%fused_computation.79 | loop fusion | flops 65536 | bytes 395520 | tf_op jit(solution)/shard_map/neg | solution.py:25
  72.8 17.3 %all-to-all-done.1 = bf16[4,1664,128]{2,1,0:T(8,128)(2,1)S(1)} async-done(((bf16[4,1664,128]{2,1,0:T(8,128)(2,1)}), bf16[4,1664,128]{2,1,0:T(8,128)(2,1)S(1)}, u32[]{:S(2)}, u32[]{:S(2)}) %all-to-all-start.1) | async-done | bytes 1703968 | tf_op jit(solution)/shard_map/all_to_all | solution.py:141
  93.2 6.8 %all-to-all-start.2 = ((bf16[128,2,384]{2,1,0:T(2,128)(2,1)}), bf16[128,2,384]{2,1,0:T(2,128)(2,1)}, u32[]{:S(2)}, u32[]{:S(2)}) async-start(bf16[128,2,384]{2,1,0:T(2,128)(2,1)} %broadcast_in_dim.42), calls=%async_computation.2 | async-start | bytes 393216 | tf_op jit(solution)/shard_map/all_to_all | solution.py:154
  100.0 1.4 fusion.25
  101.5 3.0 %collective-permute-start.4 = (bf16[256,256]{1,0:T(8,128)(2,1)S(1)}, bf16[256,256]{1,0:T(8,128)(2,1)S(1)}, u32[]{:S(2)}, u32[]{:S(2)}) collective-permute-start(bf16[256,256]{1,0:T(8,128)(2,1)S(1)} %get-tuple-element.52), channel_id=1, source_target_pairs={{0,127},{1,0},{2,1},{3,2},{4,3},{5,4},{6,5},{7,6},{8,7},{9,8},{10,... | collective-permute-start | bytes 393224 | tf_op jit(solution)/shard_map/ppermute | solution.py:15
  104.5 2.8 %collective-permute-start.3 = (bf16[256,256]{1,0:T(8,128)(2,1)S(1)}, bf16[256,256]{1,0:T(8,128)(2,1)S(1)}, u32[]{:S(2)}, u32[]{:S(2)}) collective-permute-start(bf16[256,256]{1,0:T(8,128)(2,1)S(1)} %get-tuple-element.51), channel_id=1, source_target_pairs={{0,1},{1,2},{2,3},{3,4},{4,5},{5,6},{6,7},{7,8},{8,9},{9,10},{10,1... | collective-permute-start | bytes 393224 | tf_op jit(solution)/shard_map/ppermute | solution.py:15
  114.2 1.0 reshape.170
  117.0 14.1 %all-to-all-start.3 = ((bf16[128,2,256]{2,1,0:T(2,128)(2,1)}), bf16[128,2,256]{2,1,0:T(2,128)(2,1)}, u32[]{:S(2)}, u32[]{:S(2)}) async-start(bf16[128,2,256]{2,1,0:T(2,128)(2,1)} %reshape.171), calls=%async_computation.3 | async-start | bytes 262144 | tf_op jit(solution)/shard_map/all_to_all | solution.py:179
  131.1 2.0 %fusion.102 = (f32[512]{0:T(512)S(1)}, f32[512,1024]{1,0:T(8,128)S(1)}) fusion(bf16[512,128]{1,0:T(8,128)(2,1)S(1)} %get-tuple-element.8, bf16[1024,256]{1,0:T(8,128)(2,1)} %copy-done.3, pred[1024]{0:T(1024)(128)(4,1)S(1)} %not.7, s32[512]{0:T(512)S(1)} %copy-done.11, s32[512]{0:T(512)S(1)} %fusion.54, s32[1024]{0:T(1024)S(1)} %fusion.50, ...), kind=kOutput, calls=%fused_computation.232 | convolution fusion | flops 138411520 | bytes 2502656 | tf_op jit(solution)/shard_map/qd,kd->qk/dot_general | solution.py:206
  134.8 8.7 %all-to-all-done.3 = bf16[128,2,256]{2,1,0:T(2,128)(2,1)} async-done(((bf16[128,2,256]{2,1,0:T(2,128)(2,1)}), bf16[128,2,256]{2,1,0:T(2,128)(2,1)}, u32[]{:S(2)}, u32[]{:S(2)}) %all-to-all-start.3) | async-done | bytes 131104 | tf_op jit(solution)/shard_map/all_to_all | solution.py:179
  143.5 1.0 convert_element_type.263
  145.9 1.0 copy.33
  147.9 5.5 %all-to-all-start.4 = ((bf16[128,2,128]{2,1,0:T(2,128)(2,1)}), bf16[128,2,128]{2,1,0:T(2,128)(2,1)S(1)}, u32[]{:S(2)}, u32[]{:S(2)}) async-start(bf16[128,2,128]{2,1,0:T(2,128)(2,1)} %broadcast_in_dim.46), calls=%async_computation.4 | async-start | bytes 131072 | tf_op jit(solution)/shard_map/all_to_all | solution.py:184
  153.4 1.7 fusion.13
  155.1 9.9 %all-to-all-done.4 = bf16[128,2,128]{2,1,0:T(2,128)(2,1)S(1)} async-done(((bf16[128,2,128]{2,1,0:T(2,128)(2,1)}), bf16[128,2,128]{2,1,0:T(2,128)(2,1)S(1)}, u32[]{:S(2)}, u32[]{:S(2)}) %all-to-all-start.4) | async-done | bytes 65568 | tf_op jit(solution)/shard_map/all_to_all | solution.py:184
  165.2 11.4 %all_to_all.30 = bf16[4,512,128]{1,2,0:T(8,128)(2,1)S(1)} all-to-all(bf16[4,512,128]{1,2,0:T(8,128)(2,1)S(1)} %stack.27), channel_id=1, replica_groups=mesh['section'=4,'seq'=128] {'section'}, dimensions={0} | all-to-all | bytes 1048576 | tf_op jit(solution)/shard_map/all_to_all | solution.py:229
  176.6 1.7 convolution_convert_fusion
  (131 shorter events, 21.8 us)
Async XLA Ops:
  0.0 176.6 %copy-start = (bf16[512,1024]{1,0:T(8,128)(2,1)S(1)}, bf16[512,1024]{1,0:T(8,128)(2,1)}, u32[]{:S(2)}) copy-start(bf16[512,1024]{1,0:T(8,128)(2,1)} %param.13) | copy-start | bytes 3145732
  0.0 13.1 %copy-start.1 = (bf16[512,1024]{1,0:T(8,128)(2,1)S(1)}, bf16[512,1024]{1,0:T(8,128)(2,1)}, u32[]{:S(2)}) copy-start(bf16[512,1024]{1,0:T(8,128)(2,1)} %param.8) | copy-start | bytes 3145732
  0.0 10.8 %copy-start.9 = (s32[2]{0:T(128)S(1)}, s32[2]{0:T(128)}, u32[]{:S(2)}) copy-start(s32[2]{0:T(128)} %param.15) | copy-start | bytes 28
  3.0 36.4 %collective-permute-start.2 = (bf16[1032,128]{1,0:T(8,128)(2,1)S(1)}, bf16[1032,128]{1,0:T(8,128)(2,1)}, u32[]{:S(2)}, u32[]{:S(2)}) collective-permute-start(bf16[1032,128]{1,0:T(8,128)(2,1)S(1)} %concatenate.78), channel_id=1, source_target_pairs={{0,384},{128,0},{256,128},{384,256},{1,385},{129,1},{257,129},{385... | collective-permute-start | bytes 792584 | tf_op jit(solution)/shard_map/ppermute | solution.py:15
  8.4 31.8 %collective-permute-start.1 = (bf16[1032,128]{1,0:T(8,128)(2,1)S(1)}, bf16[1032,128]{1,0:T(8,128)(2,1)}, u32[]{:S(2)}, u32[]{:S(2)}) collective-permute-start(bf16[1032,128]{1,0:T(8,128)(2,1)S(1)} %concatenate.77), channel_id=1, source_target_pairs={{0,256},{128,384},{256,0},{384,128},{1,257},{129,385},{257,1},{385... | collective-permute-start | bytes 792584 | tf_op jit(solution)/shard_map/ppermute | solution.py:15
  13.2 25.1 %copy-start.10 = (bf16[1024]{0:T(1024)(128)(2,1)S(1)}, bf16[1024]{0:T(1024)(128)(2,1)}, u32[]{:S(2)}) copy-start(bf16[1024]{0:T(1024)(128)(2,1)} %param.9) | copy-start | bytes 6148
  14.6 38.8 %all-to-all-start = ((bf16[128,2,1024]{2,1,0:T(2,128)(2,1)}), bf16[128,2,1024]{2,1,0:T(2,128)(2,1)}, u32[]{:S(2)}, u32[]{:S(2)}) async-start(bf16[128,2,1024]{2,1,0:T(2,128)(2,1)} %copy.31), calls=%async_computation | async-start | bytes 1048576 | tf_op jit(solution)/shard_map/all_to_all | solution.py:76
  33.4 10.1 %collective-permute-start = (bf16[1032,128]{1,0:T(8,128)(2,1)S(1)}, bf16[1032,128]{1,0:T(8,128)(2,1)}, u32[]{:S(2)}, u32[]{:S(2)}) collective-permute-start(bf16[1032,128]{1,0:T(8,128)(2,1)S(1)} %concatenate.76), channel_id=1, source_target_pairs={{0,128},{128,256},{256,384},{384,0},{1,129},{129,257},{257,385},{3... | collective-permute-start | bytes 792584 | tf_op jit(solution)/shard_map/ppermute | solution.py:15
  58.5 1.6 copy-start.16
  60.1 1.0 copy-start.17
  63.9 5.7 %copy-start.15 = (s32[4]{0:T(128)S(1)}, s32[4]{0:T(128)}, u32[]{:S(2)}) copy-start(s32[4]{0:T(128)} %param.14) | copy-start | bytes 52
  63.9 6.3 %copy-start.12 = (f32[2]{0:T(128)S(1)}, f32[2]{0:T(128)}, u32[]{:S(2)}) copy-start(f32[2]{0:T(128)} %get-tuple-element.83) | copy-start | bytes 28
  63.9 26.2 %all-to-all-start.1 = ((bf16[4,1664,128]{2,1,0:T(8,128)(2,1)}), bf16[4,1664,128]{2,1,0:T(8,128)(2,1)S(1)}, u32[]{:S(2)}, u32[]{:S(2)}) async-start(bf16[4,1664,128]{2,1,0:T(8,128)(2,1)} %pad_maximum_fusion), calls=%async_computation.1 | async-start | bytes 3407872 | tf_op jit(solution)/shard_map/all_to_all | solution.py:141
  90.3 9.6 %copy-start.4 = (f32[512,64]{1,0:T(8,128)S(1)}, f32[512,64]{1,0:T(8,128)}, u32[]{:S(2)}) copy-start(f32[512,64]{1,0:T(8,128)} %get-tuple-element.62) | copy-start | bytes 393220
  90.4 9.6 %copy-start.5 = (f32[512,64]{1,0:T(8,128)S(1)}, f32[512,64]{1,0:T(8,128)}, u32[]{:S(2)}) copy-start(f32[512,64]{1,0:T(8,128)} %get-tuple-element.63) | copy-start | bytes 393220
  90.4 9.6 %copy-start.6 = (f32[512,64]{1,0:T(8,128)S(1)}, f32[512,64]{1,0:T(8,128)}, u32[]{:S(2)}) copy-start(f32[512,64]{1,0:T(8,128)} %get-tuple-element.64) | copy-start | bytes 393220
  93.2 21.0 %all-to-all-start.2 = ((bf16[128,2,384]{2,1,0:T(2,128)(2,1)}), bf16[128,2,384]{2,1,0:T(2,128)(2,1)}, u32[]{:S(2)}, u32[]{:S(2)}) async-start(bf16[128,2,384]{2,1,0:T(2,128)(2,1)} %broadcast_in_dim.42), calls=%async_computation.2 | async-start | bytes 393216 | tf_op jit(solution)/shard_map/all_to_all | solution.py:154
  101.4 14.6 %copy-start.13 = (pred[128]{0:T(512)(128)(4,1)S(1)}, pred[128]{0:T(512)(128)(4,1)}, u32[]{:S(2)}) copy-start(pred[128]{0:T(512)(128)(4,1)} %get-tuple-element.100) | copy-start | bytes 388
  101.5 14.6 %copy-start.14 = (pred[128]{0:T(512)(128)(4,1)S(1)}, pred[128]{0:T(512)(128)(4,1)}, u32[]{:S(2)}) copy-start(pred[128]{0:T(512)(128)(4,1)} %get-tuple-element.101) | copy-start | bytes 388
  101.5 11.1 %collective-permute-start.4 = (bf16[256,256]{1,0:T(8,128)(2,1)S(1)}, bf16[256,256]{1,0:T(8,128)(2,1)S(1)}, u32[]{:S(2)}, u32[]{:S(2)}) collective-permute-start(bf16[256,256]{1,0:T(8,128)(2,1)S(1)} %get-tuple-element.52), channel_id=1, source_target_pairs={{0,127},{1,0},{2,1},{3,2},{4,3},{5,4},{6,5},{7,6},{8,7},{9,8},{10,... | collective-permute-start | bytes 393224 | tf_op jit(solution)/shard_map/ppermute | solution.py:15
  104.5 8.1 %collective-permute-start.3 = (bf16[256,256]{1,0:T(8,128)(2,1)S(1)}, bf16[256,256]{1,0:T(8,128)(2,1)S(1)}, u32[]{:S(2)}, u32[]{:S(2)}) collective-permute-start(bf16[256,256]{1,0:T(8,128)(2,1)S(1)} %get-tuple-element.51), channel_id=1, source_target_pairs={{0,1},{1,2},{2,3},{3,4},{4,5},{5,6},{6,7},{7,8},{8,9},{9,10},{10,1... | collective-permute-start | bytes 393224 | tf_op jit(solution)/shard_map/ppermute | solution.py:15
  112.7 0.8 copy-start.3
  113.5 17.6 %copy-start.11 = (s32[512]{0:T(512)S(1)}, s32[512]{0:T(512)}, u32[]{:S(2)}) copy-start(s32[512]{0:T(512)} %broadcast_bitcast_fusion) | copy-start | bytes 6148
  115.2 1.9 %copy-start.7 = (bf16[256,384]{1,0:T(8,128)(2,1)}, bf16[256,384]{1,0:T(8,128)(2,1)S(1)}, u32[]{:S(2)}) copy-start(bf16[256,384]{1,0:T(8,128)(2,1)S(1)} %reshape.170) | copy-start | bytes 589828
  117.0 26.4 %all-to-all-start.3 = ((bf16[128,2,256]{2,1,0:T(2,128)(2,1)}), bf16[128,2,256]{2,1,0:T(2,128)(2,1)}, u32[]{:S(2)}, u32[]{:S(2)}) async-start(bf16[128,2,256]{2,1,0:T(2,128)(2,1)} %reshape.171), calls=%async_computation.3 | async-start | bytes 262144 | tf_op jit(solution)/shard_map/all_to_all | solution.py:179
  131.1 2.0 %copy-start.8 = (bf16[256,384]{1,0:T(8,128)(2,1)S(1)}, bf16[256,384]{1,0:T(8,128)(2,1)}, u32[]{:S(2)}) copy-start(bf16[256,384]{1,0:T(8,128)(2,1)} %copy-done.7) | copy-start | bytes 589828
  133.5 0.8 copy-start.2
  134.3 19.1 %slice-start = ((bf16[256,384]{1,0:T(8,128)(2,1)}), bf16[256,128]{1,0:T(8,128)(2,1)S(1)}, s32[]{:S(2)}) async-start(bf16[256,384]{1,0:T(8,128)(2,1)} %copy-done.7), calls=%async_computation.6 | async-start | bytes 131072 | tf_op jit(solution)/shard_map/slice | solution.py:162
  147.9 17.0 %all-to-all-start.4 = ((bf16[128,2,128]{2,1,0:T(2,128)(2,1)}), bf16[128,2,128]{2,1,0:T(2,128)(2,1)S(1)}, u32[]{:S(2)}, u32[]{:S(2)}) async-start(bf16[128,2,128]{2,1,0:T(2,128)(2,1)} %broadcast_in_dim.46), calls=%async_computation.4 | async-start | bytes 131072 | tf_op jit(solution)/shard_map/all_to_all | solution.py:184
